TPU v7x, 128 devices: a whole 4x4x4 slice. The times are simulated.
128 devices in a mesh: dp: 8 (over z_lo, x), mp: 16 (over z_hi, y, core).
Axes of the slice: x: 4, y: 4, z: 4 (z_hi: 2, z_lo: 2; z = z_hi * 2 + z_lo), core: 2. Of those that a mesh axis runs over, the one named last changes fastest.
Arguments:
- tokens: bfloat16 [3072, 1024], P('dp', 'mp'), may hold values from -6 to 6
- grad_out: bfloat16 [3072, 1024], P('dp', 'mp'), may hold values from -6 to 6
- hidden_pre: bfloat16 [3072, 65536], P('dp', 'mp'), may hold values from -6 to 6
- w_in: bfloat16 [1024, 65536], P(None, 'mp'), may hold values from -0.1875 to 0.1875
- w_out: bfloat16 [65536, 1024], P('mp'), may hold values from -0.0234375 to 0.0234375
- row_in: float32 [1024], P('dp'), may hold values from 1 to 100
- col_in: float32 [65536], P('mp'), may hold values from 1 to 100
- row_out: float32 [65536], P('mp'), may hold values from 30 to 3000
- col_out: float32 [1024], P('dp'), may hold values from 30 to 3000
Outputs:
- grad_tokens: bfloat16 [3072, 1024], P('dp', 'mp')
- step_in: float32 [1024, 65536], P('dp', 'mp')
- step_out: float32 [65536, 1024], P('mp', 'dp')
- new_row_in: float32 [1024], P('dp')
- new_col_in: float32 [65536], P('mp')
- new_row_out: float32 [65536], P('mp')
- new_col_out: float32 [1024], P('dp')
All inputs are finite; a program needn't handle non-finite values.
Results may differ from a plain program's by a relative error of at most 0.0049.
Values may be sent and summed in bfloat16 or wider, within the bound.
A program may use at most 192 MiB of HBM per device.

v0:
```python
import jax
import jax.numpy as jnp
from jax import lax
from jax.sharding import PartitionSpec as P


def precondition(grads, row_acc, col_acc):
    nu = jnp.minimum(row_acc[:, None], col_acc[None, :]) + grads * grads
    return (grads / jnp.sqrt(nu), jnp.max(nu, axis=1), jnp.max(nu, axis=0))


def contract_rows(left, right):
    return lax.dot_general(
        left, right, (((0,), (0,)), ((), ())), preferred_element_type=jnp.float32
    )


def on_device(tokens, grad_out, hidden_pre, w_in, w_out, row_in, col_in, row_out, col_out):
    x_full, dy_full = (
        lax.all_gather(tokens, "mp", axis=1, tiled=True),
        lax.all_gather(grad_out, "mp", axis=1, tiled=True),
    )
    relu_out = jnp.maximum(hidden_pre, jnp.zeros_like(hidden_pre))
    back = lax.dot_general(
        dy_full, w_out, (((1,), (1,)), ((), ())), preferred_element_type=jnp.float32
    )
    hidden_grad = jnp.where(hidden_pre > 0, back, jnp.float32(0.0)).astype(jnp.bfloat16)
    input_term = lax.dot_general(
        hidden_grad, w_in, (((1,), (1,)), ((), ())), preferred_element_type=jnp.float32
    )
    grad_tokens = lax.psum_scatter(input_term, "mp", scatter_dimension=1, tiled=True).astype(
        jnp.bfloat16
    )
    width = w_in.shape[1]
    first = contract_rows(x_full, hidden_grad)
    second = contract_rows(dy_full, relu_out)
    summed = lax.psum_scatter(
        jnp.concatenate([first, second], axis=1), "dp", scatter_dimension=0, tiled=True
    )
    grad_in = summed[:, :width]
    grad_out_t = summed[:, width:]
    step_in, rowmax_in, colmax_in = precondition(grad_in, row_in, col_in)
    step_out_t, peak_model, peak_hidden = precondition(grad_out_t, col_out, row_out)
    new_row_in, new_col_out = lax.pmax((rowmax_in, peak_model), "mp")
    new_col_in, new_row_out = lax.pmax((colmax_in, peak_hidden), "dp")
    return (grad_tokens, step_in, step_out_t.T, new_row_in, new_col_in, new_row_out, new_col_out)


def solution(mesh):
    in_specs = (
        P("dp", "mp"),
        P("dp", "mp"),
        P("dp", "mp"),
        P(None, "mp"),
        P("mp", None),
        P("dp"),
        P("mp"),
        P("mp"),
        P("dp"),
    )
    out_specs = (P("dp", "mp"), P("dp", "mp"), P("mp", "dp"), P("dp"), P("mp"), P("mp"), P("dp"))
    return jax.shard_map(
        on_device, mesh=mesh, in_specs=in_specs, out_specs=out_specs, check_vma=False
    )
```

profile of v0, /device:TPU:0, one launch (start us, length us, event | category | flops | bytes accessed | tf_op | source)
XLA Modules:
  0.0 532.1 jit_solution(12049669624587012981)
XLA Ops:
  7.2 0.0 reduce-scatter.3.cloned.1.call-start
  7.2 0.0 slice-start
  7.2 27.9 %all_gather.6 = bf16[384,1024]{0,1:T(8,128)(2,1)S(1)} all-gather(bf16[384,64]{0,1:T(8,128)(2,1)} %param.10), channel_id=1, replica_groups=mesh['dp'=8,'mp'=16] {'mp'}, dimensions={1}, use_global_device_ids=true | all-gather | bytes 835584 | tf_op jit(solution)/shard_map/all_gather | solution.py:21
  35.1 0.0 copy-start
  35.1 0.0 slice-start.1
  35.1 9.9 %select_convert_fusion = bf16[384,4096]{1,0:T(8,128)(2,1)} fusion(bf16[384,4096]{1,0:T(8,128)(2,1)} %param.11, bf16[384,1024]{0,1:T(8,128)(2,1)S(1)} %all_gather.6, bf16[4096,1024]{1,0:T(8,128)(2,1)} %param.13), kind=kOutput, calls=%fused_computation.3 | convolution fusion | flops 3225944064 | bytes 15466496 | tf_op jit(solution)/shard_map/dot_general | solution.py:24
  45.0 0.0 copy-done
  45.0 0.0 slice-done
  45.0 0.0 slice-done.1
  45.0 7.6 %fusion.7 = f32[384,1024]{0,1:T(8,128)} fusion(bf16[384,4096]{1,0:T(8,128)(2,1)} %select_convert_fusion, bf16[1024,4096]{1,0:T(8,128)(2,1)S(1)} %bitcast.14), kind=kOutput, calls=%fused_computation.15 | convolution fusion | flops 3221225472 | bytes 13107200 | tf_op jit(solution)/shard_map/dot_general | solution.py:28
  52.7 0.0 reduce-scatter.3.cloned.1.call-update
  52.7 0.0 copy-start.1
  52.7 0.0 reduce-scatter.5.cloned.1.call-start
  52.7 6.7 %convolution_bitcast_fusion = f32[1024,4096]{0,1:T(8,128)S(1)} fusion(bf16[384,1024]{0,1:T(8,128)(2,1)} %copy-done, bf16[384,4096]{1,0:T(8,128)(2,1)} %param.11), kind=kOutput, calls=%fused_computation.1 | convolution fusion | flops 3222798336 | bytes 20709376 | tf_op jit(solution)/shard_map/dot_general | solution.py:13
  59.4 0.0 copy-done.1
  59.4 23.0 %all_gather.7 = bf16[384,1024]{0,1:T(8,128)(2,1)} all-gather(bf16[384,64]{0,1:T(8,128)(2,1)S(1)} %copy-done.1), channel_id=1, replica_groups=mesh['dp'=8,'mp'=16] {'mp'}, dimensions={1}, use_global_device_ids=true | all-gather | bytes 835584 | tf_op jit(solution)/shard_map/all_gather | solution.py:20
  82.5 6.7 %convolution_bitcast_fusion.1 = f32[1024,4096]{0,1:T(8,128)S(1)} fusion(bf16[384,4096]{1,0:T(8,128)(2,1)} %select_convert_fusion, bf16[384,1024]{0,1:T(8,128)(2,1)} %all_gather.7), kind=kOutput, calls=%fused_computation.2 | convolution fusion | flops 3221225472 | bytes 20709376 | tf_op jit(solution)/shard_map/dot_general | solution.py:13
  89.2 12.6 %pad_maximum_fusion = f32[1024,8192]{0,1:T(8,128)} fusion(f32[1024,4096]{0,1:T(8,128)S(1)} %convolution_bitcast_fusion, f32[1024,4096]{0,1:T(8,128)S(1)} %convolution_bitcast_fusion.1), kind=kLoop, calls=%fused_computation | loop fusion | flops 8388608 | bytes 67108864 | tf_op jit(solution)/shard_map/concatenate | solution.py:38
  101.8 0.0 copy-start.2
  101.8 0.0 copy-start.3
  101.8 0.0 reduce-scatter.5.cloned.1.call-update
  101.8 16.7 %reduce-scatter.3.cloned.1.call-done = f32[384,64]{0,1:T(8,128)} async-done(((f32[384,1024]{0,1:T(8,128)}), f32[384,64]{0,1:T(8,128)}) %reduce-scatter.3.cloned.1.call-update) | async-done | bytes 98320 | tf_op jit(solution)/shard_map/reduce_scatter | solution.py:31
  118.5 1.5 convert_element_type.7
  120.0 328.6 %reduce-scatter.5.cloned.1.call-done = f32[128,8192]{0,1:T(8,128)} async-done(((f32[1024,8192]{0,1:T(8,128)}), f32[128,8192]{0,1:T(8,128)}) %reduce-scatter.5.cloned.1.call-update) | async-done | bytes 4194320 | tf_op jit(solution)/shard_map/reduce_scatter | solution.py:37
  448.6 0.0 copy-done.2
  448.6 0.0 copy-done.3
  448.6 0.0 copy-done.4
  448.6 0.0 copy-done.5
  448.6 5.2 fusion.1
  453.8 1.8 copy.16
  455.6 38.2 %all-reduce = (f32[128]{0:T(128)}, f32[128]{0:T(128)}) all-reduce(f32[128]{0:T(128)S(1)} %get-tuple-element.18, f32[128]{0:T(128)S(1)} %get-tuple-element.14), channel_id=1, replica_groups=mesh['dp'=8,'mp'=16] {'mp'}, use_global_device_ids=true, to_apply=%region_3.4 | all-reduce | flops 256 | bytes 2048 | tf_op jit(solution)/shard_map/pmax | solution.py:44
  493.8 31.5 %all-reduce.1 = (f32[4096]{0:T(1024)}, f32[4096]{0:T(1024)}) all-reduce(f32[4096]{0:T(1024)S(1)} %get-tuple-element.19, f32[4096]{0:T(1024)S(1)} %get-tuple-element.15), channel_id=1, replica_groups=mesh['dp'=8,'mp'=16] {'dp'}, use_global_device_ids=true, to_apply=%region_5.6 | all-reduce | flops 8192 | bytes 65536 | tf_op jit(solution)/shard_map/pmax | solution.py:45
  (3 shorter events, 0.0 us)
Async XLA Ops:
  7.2 111.3 %reduce-scatter.3.cloned.1.call-start = ((), (), s32[]{:S(2)}) async-start(), calls=%async_computation.2 | async-start | bytes 1671168 | tf_op jit(solution)/shard_map/reduce_scatter | solution.py:31
  7.2 37.8 %slice-start = ((s8[8388608]{0:T(1024)(128)(4,1)}), s8[4194304]{0:T(1024)(128)(4,1)S(1)}, s32[]{:S(2)}) async-start(s8[8388608]{0:T(1024)(128)(4,1)} %bitcast.13), calls=%async_computation.4 | async-start | bytes 8388608
  35.1 9.9 %copy-start = (bf16[384,1024]{0,1:T(8,128)(2,1)}, bf16[384,1024]{0,1:T(8,128)(2,1)S(1)}, u32[]{:S(2)}) copy-start(bf16[384,1024]{0,1:T(8,128)(2,1)S(1)} %all_gather.6) | copy-start | bytes 2359300
  35.1 9.9 %slice-start.1 = ((s8[8388608]{0:T(1024)(128)(4,1)}), s8[4194304]{0:T(1024)(128)(4,1)S(1)}, s32[]{:S(2)}) async-start(s8[8388608]{0:T(1024)(128)(4,1)} %bitcast.13), calls=%async_computation.5 | async-start | bytes 8388608
  52.7 6.8 %copy-start.1 = (bf16[384,64]{0,1:T(8,128)(2,1)S(1)}, bf16[384,64]{0,1:T(8,128)(2,1)}, u32[]{:S(2)}) copy-start(bf16[384,64]{0,1:T(8,128)(2,1)} %param.9) | copy-start | bytes 147460
  52.7 395.9 %reduce-scatter.5.cloned.1.call-start = ((), (), s32[]{:S(2)}) async-start(), calls=%async_computation.3 | async-start | bytes 37748736 | tf_op jit(solution)/shard_map/reduce_scatter | solution.py:37
  101.8 346.8 %copy-start.2 = (f32[4096]{0:T(1024)S(1)}, f32[4096]{0:T(1024)}, u32[]{:S(2)}) copy-start(f32[4096]{0:T(1024)} %param.16) | copy-start | bytes 49156
  101.8 346.8 %copy-start.3 = (f32[4096]{0:T(1024)S(1)}, f32[4096]{0:T(1024)}, u32[]{:S(2)}) copy-start(f32[4096]{0:T(1024)} %param.15) | copy-start | bytes 49156
  101.8 346.8 %copy-start.4 = (f32[128]{0:T(128)S(1)}, f32[128]{0:T(128)}, u32[]{:S(2)}) copy-start(f32[128]{0:T(128)} %param.17) | copy-start | bytes 1540
  101.8 346.8 %copy-start.5 = (f32[128]{0:T(128)S(1)}, f32[128]{0:T(128)}, u32[]{:S(2)}) copy-start(f32[128]{0:T(128)} %param.14) | copy-start | bytes 1540
Sparse Core Ops, SparseCore 0:
  52.8 65.6 reduce-scatter.2
  121.0 327.5 reduce-scatter.4
where the time goes:
time: 532 us
  waiting for transfers between devices  345 us (65%)
  blocking collectives  120 us (23%)
  matrix products  31 us (6%)
  other arithmetic  19.4 us (4%)
  between operations  14.1 us (3%)
    reduce_scatter x1, waiting for transfers between devices, on_device(): lax.psum_scatter(jnp.concatenate([first, second], axis=1), 'dp', scatter_...  329 us
    pmax x1, blocking collectives, on_device(): new_row_in, new_col_out = lax.pmax((rowmax_in, peak_model), 'mp')  38.2 us
    pmax x1, blocking collectives, on_device(): new_col_in, new_row_out = lax.pmax((colmax_in, peak_hidden), 'dp')  31.5 us
    all_gather x1, blocking collectives, on_device(): lax.all_gather(grad_out, 'mp', axis=1, tiled=True)  27.9 us
    all_gather x1, blocking collectives, on_device(): lax.all_gather(tokens, 'mp', axis=1, tiled=True)  23 us
    reduce_scatter x1, waiting for transfers between devices, on_device(): lax.psum_scatter(input_term, 'mp', scatter_dimension=1, tiled=True)  16.7 us
    dot_general x2, matrix products, contract_rows(): lax.dot_general(left, right, (((0,), (0,)), ((), ())), preferred_element_...  13.4 us
    concatenate x1, other arithmetic, on_device(): jnp.concatenate([first, second], axis=1)  12.6 us
  transfers between devices with their start and end apart: 2, of which 2 were waited for; matrix products, arithmetic and copies ran while one was open for 5% of the time, Pallas kernels for 0%

commit v1 on v0

v1 whole, which is shorter than its diff:
```python
import jax
import jax.numpy as jnp
from jax import lax
from jax.experimental import pallas as pl
from jax.experimental.pallas import tpu as pltpu
from jax.sharding import PartitionSpec as P

MESH = pl.DeviceIdType.MESH
F32, BF16 = jnp.float32, jnp.bfloat16

TOK = 384
FF = 4096
D = 1024
W = 256
K = FF // W
DELTA = 2
LAG_D = 1
LAG_F = 3
RING = 4
AHEAD = 3
HALF = K // 2


def nt(left, right):
    return lax.dot_general(left, right, (((1,), (1,)), ((), ())), preferred_element_type=F32)


def kernel(
    blk, hid_hbm, win_hbm, wout_hbm, row_in, col_in, row_out, col_out,
    gt_out, step_in, step_out, new_row_in, new_col_in, new_row_out, new_col_out,
    hid, win, wout, gath, dy, lhs, hgo, hgb, gtacc,
    f_send, f_recv, n_send, n_recv, d_send, d_recv, keep_d, keep_0,
    gs1, gr1, gs2, gk2, gr2, gs3, gk3, gr3,
    rb, rowm, colm, colr, colm2, colr2, rm1, rr1, rm2, rr2, rm3, rr3,
    load_sem, z_ss, z_rs, s_ss, s_rs, y_ss, y_rs, c_ss, c_rs,
    f_ss, f_rs, n_ss, n_rs, d_ss, d_rs, g_ss, g_rs, e_ss, e_rs,
):
    dp = lax.axis_index("dp")
    mp = lax.axis_index("mp")
    zlo, x = dp // 4, dp % 4
    zhi, y, c = mp // 8, (mp // 2) % 4, mp % 2

    def dev(zlo_, x_, zhi_, y_, c_):
        return (zlo_ * 4 + x_, zhi_ * 8 + y_ * 2 + c_)

    x_peer = [dev(zlo, (x + i) % 4, zhi, y, c) for i in range(4)]
    y_peer = [dev(zlo, x, zhi, (y + i) % 4, c) for i in range(4)]
    zlo_peer = dev(1 - zlo, x, zhi, y, c)
    zhi_peer = dev(zlo, x, 1 - zhi, y, c)
    diag_peer = dev(1 - zlo, x, 1 - zhi, y, c)
    core_peer = dev(zlo, x, zhi, y, 1 - c)

    def remote(src, dst, ss, rs, peer):
        return pltpu.make_async_remote_copy(
            src_ref=src, dst_ref=dst, send_sem=ss, recv_sem=rs, device_id=peer, device_id_type=MESH
        )

    loads = [
        pltpu.make_async_copy(hid_hbm, hid.at[pl.ds(zlo * TOK, TOK)], load_sem.at[0]),
        pltpu.make_async_copy(wout_hbm, wout, load_sem.at[1]),
        pltpu.make_async_copy(win_hbm, win, load_sem.at[2]),
    ]
    for load in loads:
        load.start()

    barrier = pltpu.get_barrier_semaphore()
    peers = x_peer[1:] + y_peer[1:] + [zlo_peer, zhi_peer, diag_peer, core_peer]
    for peer in peers:
        pl.semaphore_signal(barrier, inc=1, device_id=peer, device_id_type=MESH)
    pl.semaphore_wait(barrier, len(peers))

    piece = gath.at[zhi, y, c, zlo]
    s1 = remote(blk, piece, s_ss.at[0], s_rs.at[0], zlo_peer)
    s2 = remote(blk, piece, s_ss.at[1], s_rs.at[1], diag_peer)
    s1.start()
    s2.start()

    def z_copy(k):
        cols = pl.ds(pl.multiple_of(k * W, W), W)
        return remote(
            hid_hbm.at[:, cols], hid.at[pl.ds(zlo * TOK, TOK), cols], z_ss.at[k], z_rs.at[k], zlo_peer
        )

    for k in range(AHEAD):
        z_copy(k).start()
    piece[...] = blk[...]
    s1.wait_recv()
    other = gath.at[zhi, y, c, 1 - zlo]
    s3 = remote(other, other, s_ss.at[2], s_rs.at[2], diag_peer)
    s3.start()
    s2.wait_recv()
    s3.wait_recv()

    def rows_of(stage):
        return (zlo, pl.ds(64, 64)) if stage == 0 else (zlo, pl.ds(0, 64)) if stage == 1 else (1 - zlo, pl.ds(64, 64))

    def y_copy(stage, i):
        h, rows = rows_of(stage)
        part = gath.at[h, y, c, :, rows]
        return remote(part, part, y_ss.at[stage, i - 1], y_rs.at[stage, i - 1], y_peer[i])

    def c_copy(stage):
        h, rows = rows_of(stage)
        part = gath.at[h, :, c, :, rows]
        return remote(part, part, c_ss.at[stage], c_rs.at[stage], core_peer)

    for stage in range(3):
        for i in (1, 3, 2):
            y_copy(stage, i).start()

    def row_block(row):
        return jnp.broadcast_to(row[...], (128, 128)).T

    rb[0] = row_block(row_in)
    rb[1] = row_block(col_out)
    rowm[...] = jnp.zeros_like(rowm)

    def finish_gather(stage):
        for i in (1, 2, 3):
            y_copy(stage, i).wait_recv()
        c_copy(stage).start()
        c_copy(stage).wait_recv()

    def assemble(mat):
        for r in range(4):
            owner = (x + r) % 4
            for core in range(2):
                for lo in range(2):
                    lhs[mat, pl.ds(r * 128 + core * 64, 64), pl.ds(lo * TOK, TOK)] = gath[
                        zlo, owner, core, lo, pl.ds(64 * mat, 64), :
                    ]

    def transpose_dy():
        for h in range(2):
            for yy in range(4):
                for lo in range(2):
                    both = jnp.concatenate(
                        [gath[h, yy, 0, lo, 64:128, :], gath[h, yy, 1, lo, 64:128, :]], axis=0
                    )
                    dy[pl.ds(lo * TOK, TOK), pl.ds((h * 4 + yy) * 128, 128)] = both.astype(F32).T.astype(BF16)

    finish_gather(0)
    assemble(1)
    loads[0].wait()
    loads[1].wait()

    toward = [(x_peer[1], x_peer[3]), (x_peer[3], x_peer[1])]

    def f_copy(mat, k):
        return remote(f_send.at[mat, k], f_recv.at[mat, k], f_ss.at[mat, k], f_rs.at[mat, k], toward[mat][0])

    def n_copy(mat, k):
        return remote(n_send.at[mat, k], n_recv.at[mat, k], n_ss.at[mat, k], n_rs.at[mat, k], toward[mat][1])

    def d_copy(mat, k):
        return remote(d_send.at[mat, k], d_recv.at[mat, k], d_ss.at[mat, k], d_rs.at[mat, k], toward[mat][0])

    def products(mat, k, right):
        part = jnp.dot(lhs[mat], right, preferred_element_type=F32)
        near, back = (3, 1) if mat == 0 else (1, 3)
        slot = k % RING
        f_send[mat, k] = part[256:384].astype(BF16)
        f_copy(mat, k).start()
        n_send[mat, k] = part[near * 128 : near * 128 + 128].astype(BF16)
        n_copy(mat, k).start()
        keep_d[mat, slot] = part[back * 128 : back * 128 + 128]
        keep_0[mat, slot] = part[0:128]

    def pass_on(mat, k):
        f_copy(mat, k).wait_recv()
        d_send[mat, k] = (keep_d[mat, k % RING] + f_recv[mat, k].astype(F32)).astype(BF16)
        d_copy(mat, k).start()

    def finish(mat, k):
        n_copy(mat, k).wait_recv()
        d_copy(mat, k).wait_recv()
        lanes = col_in if mat == 0 else row_out
        for h in range(W // 128):
            cut = pl.ds(h * 128, 128)
            g = (
                keep_0[mat, k % RING, :, cut]
                + n_recv[mat, k, :, cut].astype(F32)
                + d_recv[mat, k, :, cut].astype(F32)
            )
            block = k * (W // 128) + h
            nu = jnp.minimum(rb[mat], lanes[pl.ds(block, 1), :]) + g * g
            step = g * lax.rsqrt(nu)
            at = pl.ds(pl.multiple_of(block * 128, 128), 128)
            if mat == 0:
                step_in[:, at] = step
            else:
                step_out[at, :] = step.T
            rowm[mat] = jnp.maximum(rowm[mat], nu)
            colm[pl.ds(mat * (FF // 128) + block, 1), :] = jnp.max(nu, axis=0, keepdims=True)
        f_copy(mat, k).wait_send()
        n_copy(mat, k).wait_send()
        d_copy(mat, k).wait_send()

    def hidden_grad(lo, k):
        cols = pl.ds(pl.multiple_of(k * W, W), W)
        rows = pl.ds(pl.multiple_of(lo * TOK, TOK), TOK)
        back = nt(dy[rows, :], wout[cols, :])
        return jnp.where(hid[rows, cols] > 0, back, F32(0.0)).astype(BF16)

    def own_tokens(k):
        cols = pl.ds(pl.multiple_of(k * W, W), W)
        grad = hidden_grad(zlo, k)
        hgo[:, cols] = grad
        gtacc[...] += nt(win[:, cols], grad)

    def g_copy(i):
        if i == 0:
            return remote(gs1, gr1, g_ss.at[0], g_rs.at[0], core_peer)
        if i < 4:
            return remote(gs2.at[(y + i) % 4], gr2.at[i - 1], g_ss.at[i], g_rs.at[i], y_peer[i])
        return remote(gs3, gr3, g_ss.at[4], g_rs.at[4], zhi_peer)

    def gt_rows(j, core):
        return gtacc[pl.ds(pl.multiple_of(j * 128 + core * 64, 64), 64), :]

    def gt_stage(i):
        if i == 0:
            for j in range(8):
                gs1[j] = gt_rows(j, 1 - c).astype(BF16)
            g_copy(0).start()
        elif i == 1:
            g_copy(0).wait_recv()
            for h in range(2):
                for yy in range(4):
                    gs2[yy, h] = (gt_rows(h * 4 + yy, c) + gr1[h * 4 + yy].astype(F32)).astype(BF16)
                gk2[h] = gt_rows(h * 4 + y, c) + gr1[h * 4 + y].astype(F32)
            for j in (1, 2, 3):
                g_copy(j).start()
        elif i == 2:
            for j in (1, 2, 3):
                g_copy(j).wait_recv()

            def total(h):
                return gk2[h] + gr2[0, h].astype(F32) + gr2[1, h].astype(F32) + gr2[2, h].astype(F32)

            gs3[...] = total(1 - zhi).astype(BF16)
            gk3[...] = total(zhi)
            g_copy(4).start()
        else:
            g_copy(4).wait_recv()
            gt_out[...] = (gk3[...] + gr3[...].astype(F32)).astype(BF16)
            for j in range(5):
                g_copy(j).wait_send()

    def between(value, low, high):
        return jnp.logical_and(value >= low, value < high)

    def turn(i, carry):
        for mat, first in ((1, 0), (0, DELTA)):

            @pl.when(between(i - first - LAG_D, 0, K))
            def _():
                pass_on(mat, i - first - LAG_D)

            @pl.when(between(i - first - LAG_F, 0, K))
            def _():
                finish(mat, i - first - LAG_F)

        @pl.when(i < K)
        def _():
            z_copy(i).wait_recv()

            @pl.when(i + AHEAD < K)
            def _():
                z_copy(i + AHEAD).start()

            cols = pl.ds(pl.multiple_of(i * W, W), W)
            pre = hid[:, cols]
            products(1, i, jnp.maximum(pre, jnp.zeros_like(pre)))

        p = i - DELTA

        @pl.when(p == 0)
        def _():
            finish_gather(1)
            assemble(0)
            finish_gather(2)
            transpose_dy()
            loads[2].wait()
            gtacc[...] = jnp.zeros_like(gtacc)

        @pl.when(between(p, 0, HALF))
        def _():
            own_tokens(2 * p)
            own_tokens(2 * p + 1)

        @pl.when(between(p, 0, K))
        def _():
            cols = pl.ds(pl.multiple_of(p * W, W), W)
            hgb[pl.ds(pl.multiple_of(zlo * TOK, TOK), TOK), :] = hgo[:, cols]
            hgb[pl.ds(pl.multiple_of((1 - zlo) * TOK, TOK), TOK), :] = hidden_grad(1 - zlo, p)
            products(0, p, hgb[...])

        for s, at in enumerate((HALF, HALF + 1, HALF + 3, HALF + 5)):

            @pl.when(p == at)
            def _():
                gt_stage(s)

        return carry

    lax.fori_loop(0, K + DELTA + LAG_F, turn, 0)

    def e_copy(i):
        if i < 3:
            return remote(colm, colr.at[i], e_ss.at[i], e_rs.at[i], x_peer[i + 1])
        if i == 3:
            return remote(rm1, rr1, e_ss.at[3], e_rs.at[3], core_peer)
        if i == 4:
            return remote(colm2, colr2, e_ss.at[4], e_rs.at[4], zlo_peer)
        if i < 8:
            return remote(rm2, rr2.at[i - 5], e_ss.at[i], e_rs.at[i], y_peer[i - 4])
        return remote(rm3, rr3, e_ss.at[8], e_rs.at[8], zhi_peer)

    for i in range(3):
        e_copy(i).start()
    rm1[...] = jnp.zeros_like(rm1)
    for mat in range(2):
        rm1[mat : mat + 1, :] = jnp.max(rowm[mat].T, axis=0, keepdims=True)
    e_copy(3).start()
    e_copy(3).wait_recv()
    rm2[...] = jnp.maximum(rm1[...], rr1[...])
    for i in (5, 6, 7):
        e_copy(i).start()
    for i in range(3):
        e_copy(i).wait_recv()
    colm2[...] = jnp.maximum(jnp.maximum(colm[...], colr[0]), jnp.maximum(colr[1], colr[2]))
    e_copy(4).start()
    for i in (5, 6, 7):
        e_copy(i).wait_recv()
    rm3[...] = jnp.maximum(jnp.maximum(rm2[...], rr2[0]), jnp.maximum(rr2[1], rr2[2]))
    e_copy(8).start()
    e_copy(4).wait_recv()
    rows = FF // 128
    new_col_in[...] = jnp.maximum(colm2[0:rows], colr2[0:rows])
    new_row_out[...] = jnp.maximum(colm2[rows:], colr2[rows:])
    e_copy(8).wait_recv()
    new_row_in[...] = jnp.maximum(rm3[0:1], rr3[0:1])
    new_col_out[...] = jnp.maximum(rm3[1:2], rr3[1:2])

    for i in range(9):
        e_copy(i).wait_send()
    for copy in (s1, s2, s3):
        copy.wait_send()
    for stage in range(3):
        for i in (1, 2, 3):
            y_copy(stage, i).wait_send()
        c_copy(stage).wait_send()

    def z_sent(k, carry):
        z_copy(k).wait_send()
        return carry

    lax.fori_loop(0, K, z_sent, 0)


def on_device(tokens, grad_out, hidden_pre, w_in, w_out, row_in, col_in, row_out, col_out):
    blk = jnp.concatenate([tokens, grad_out], axis=1).T
    vmem = pl.BlockSpec(memory_space=pltpu.VMEM)
    hbm = pl.BlockSpec(memory_space=pl.ANY)
    dma = pltpu.SemaphoreType.DMA
    rows = FF // 128
    wire = pltpu.VMEM((2, K, 128, W), BF16)
    kept = pltpu.VMEM((2, RING, 128, W), F32)
    gt, step_in, step_out, nri, nci, nro, nco = pl.pallas_call(
        kernel,
        out_shape=(
            jax.ShapeDtypeStruct((64, TOK), BF16),
            jax.ShapeDtypeStruct((128, FF), F32),
            jax.ShapeDtypeStruct((FF, 128), F32),
            jax.ShapeDtypeStruct((1, 128), F32),
            jax.ShapeDtypeStruct((rows, 128), F32),
            jax.ShapeDtypeStruct((rows, 128), F32),
            jax.ShapeDtypeStruct((1, 128), F32),
        ),
        in_specs=[vmem, hbm, hbm, hbm, vmem, vmem, vmem, vmem],
        out_specs=(vmem,) * 7,
        scratch_shapes=[
            pltpu.VMEM((2 * TOK, FF), BF16),
            pltpu.VMEM((D, FF), BF16),
            pltpu.VMEM((FF, D), BF16),
            pltpu.VMEM((2, 4, 2, 2, 128, TOK), BF16),
            pltpu.VMEM((2 * TOK, D), BF16),
            pltpu.VMEM((2, 512, 2 * TOK), BF16),
            pltpu.VMEM((TOK, FF), BF16),
            pltpu.VMEM((2 * TOK, W), BF16),
            pltpu.VMEM((D, TOK), F32),
            wire, wire, wire, wire, wire, wire,
            kept, kept,
            pltpu.VMEM((8, 64, TOK), BF16),
            pltpu.VMEM((8, 64, TOK), BF16),
            pltpu.VMEM((4, 2, 64, TOK), BF16),
            pltpu.VMEM((2, 64, TOK), F32),
            pltpu.VMEM((3, 2, 64, TOK), BF16),
            pltpu.VMEM((64, TOK), BF16),
            pltpu.VMEM((64, TOK), F32),
            pltpu.VMEM((64, TOK), BF16),
            pltpu.VMEM((2, 128, 128), F32),
            pltpu.VMEM((2, 128, 128), F32),
            pltpu.VMEM((2 * rows, 128), F32),
            pltpu.VMEM((3, 2 * rows, 128), F32),
            pltpu.VMEM((2 * rows, 128), F32),
            pltpu.VMEM((2 * rows, 128), F32),
            pltpu.VMEM((8, 128), F32),
            pltpu.VMEM((8, 128), F32),
            pltpu.VMEM((8, 128), F32),
            pltpu.VMEM((3, 8, 128), F32),
            pltpu.VMEM((8, 128), F32),
            pltpu.VMEM((8, 128), F32),
            dma((3,)),
            dma((K,)), dma((K,)),
            dma((3,)), dma((3,)),
            dma((3, 3)), dma((3, 3)),
            dma((3,)), dma((3,)),
            dma((2, K)), dma((2, K)),
            dma((2, K)), dma((2, K)),
            dma((2, K)), dma((2, K)),
            dma((5,)), dma((5,)),
            dma((9,)), dma((9,)),
        ],
        compiler_params=pltpu.CompilerParams(
            collective_id=0, has_side_effects=True, vmem_limit_bytes=63 * 2**20
        ),
        name="ffn_backward",
    )(
        blk, hidden_pre, w_in, w_out,
        row_in.reshape(1, 128), col_in.reshape(rows, 128), row_out.reshape(rows, 128), col_out.reshape(1, 128),
    )
    return (
        gt.T, step_in, step_out,
        nri.reshape(128), nci.reshape(FF), nro.reshape(FF), nco.reshape(128),
    )


def solution(mesh):
    in_specs = (
        P("dp", "mp"),
        P("dp", "mp"),
        P("dp", "mp"),
        P(None, "mp"),
        P("mp", None),
        P("dp"),
        P("mp"),
        P("mp"),
        P("dp"),
    )
    out_specs = (P("dp", "mp"), P("dp", "mp"), P("mp", "dp"), P("dp"), P("mp"), P("mp"), P("dp"))
    return jax.shard_map(
        on_device, mesh=mesh, in_specs=in_specs, out_specs=out_specs, check_vma=False
    )
```

time: 532 us -> 165 us (0.31)
  waiting for transfers between devices: 345 us -> 0 us
  Pallas kernels: 0 us -> 154 us
  blocking collectives: 120 us -> 0 us
  matrix products: 31 us -> 0 us
  other arithmetic: 19.4 us -> 1.47 us
  between operations: 14.1 us -> 0.66 us
  local copies, waits for them, and re-layouts: 1.84 us -> 8.26 us
    reduce_scatter x2 -> x0, waiting for transfers between devices: 345 us -> none  [the longest x1 329 us: on_device(): lax.psum_scatter(jnp.concatenate([first, second], axis=1), 'dp', scatter_...]
    pallas_call x0 -> x1, Pallas kernels: none -> 154 us  [on_device(): pl.pallas_call(kernel, out_shape=(jax.ShapeDtypeStruct((64, TOK), BF16),...]
    pmax x2 -> x0, blocking collectives: 69.6 us -> none  [the longest x1 38.2 us: on_device(): new_row_in, new_col_out = lax.pmax((rowmax_in, peak_model), 'mp')]
    all_gather x2 -> x0, blocking collectives: 50.9 us -> none  [the longest x1 27.9 us: on_device(): lax.all_gather(grad_out, 'mp', axis=1, tiled=True)]
    dot_general x4 -> x0, matrix products: 31 us -> none  [the longest x2 13.4 us: contract_rows(): lax.dot_general(left, right, (((0,), (0,)), ((), ())), preferred_element_...]
    concatenate x1 -> x0, other arithmetic: 12.6 us -> none  [on_device(): jnp.concatenate([first, second], axis=1)]
    unnamed x17, local copies, waits for them, and re-layouts: 1.84 us -> 8.26 us
  transfers between devices with their start and end apart: 2 -> 0, of which waited for: 2 -> 0; matrix products, arithmetic and copies ran while one was open for 5% -> 0% of each run, Pallas kernels for 0% -> 0%
where the time goes in v1:
time: 165 us
  Pallas kernels  154 us (93%)
  local copies, waits for them, and re-layouts  8.26 us (5%)
    pallas_call x1, Pallas kernels, on_device(): pl.pallas_call(kernel, out_shape=(jax.ShapeDtypeStruct((64, TOK), BF16),...  154 us
    unnamed x17, local copies, waits for them, and re-layouts  8.26 us

profile of v1, /device:TPU:0, one launch (start us, length us, event | category | flops | bytes accessed | tf_op | source)
XLA Modules:
  0.0 164.8 jit_solution(10401878179427646623)
XLA Ops:
  0.6 1.5 maximum_bitcast_fusion.blk
  2.1 154.4 %ffn_backward.1 = (bf16[64,384]{1,0:T(8,128)(2,1)}, f32[128,4096]{1,0:T(8,128)}, f32[4096,128]{1,0:T(8,128)}, f32[1,128]{1,0:T(1,128)}, f32[32,128]{1,0:T(8,128)}, /*index=5*/f32[32,128]{1,0:T(8,128)}, f32[1,128]{1,0:T(1,128)}) custom-call(bf16[128,384]{1,0:T(8,128)(2,1)} %maximum_bitcast_fusion.blk, bf16[384,4096]{1,0:T(8,128)(2,1)} %hid_hbm.1, ...), custom_call_target="tpu_custom_call" | custom-call | tf_op jit(solution)/shard_map/ffn_backward/pallas_call | solution.py:370
  156.5 1.4 copy.23
  157.9 0.0 copy-start
  157.9 3.3 %copy.24 = f32[128,4096]{1,0:T(8,128)} copy(f32[128,4096]{1,0:T(8,128)} %get-tuple-element.29) | data formatting | bytes 4194304
  161.2 0.0 copy-done
  161.2 0.0 copy-start.4
  161.2 0.0 copy-start.2
  161.2 0.0 copy-start.1
  161.2 0.0 copy-start.3
  161.2 1.3 copy.25
  162.5 0.0 copy-done.4
  162.5 0.5 copy.26
  163.1 0.0 copy-done.2
  163.1 0.6 copy.27
  163.7 0.0 copy-done.1
  163.7 0.6 copy.28
  164.3 0.0 copy-done.3
  164.3 0.5 copy.29
Async XLA Ops:
  157.9 3.3 %copy-start = (f32[4096,128]{1,0:T(8,128)S(1)}, f32[4096,128]{1,0:T(8,128)}, u32[]{:S(2)}) copy-start(f32[4096,128]{1,0:T(8,128)} %get-tuple-element.30) | copy-start | bytes 6291460
  161.2 1.3 copy-start.4
  161.2 1.9 %copy-start.2 = (f32[32,128]{1,0:T(8,128)S(1)}, f32[32,128]{1,0:T(8,128)}, u32[]{:S(2)}) copy-start(f32[32,128]{1,0:T(8,128)} %get-tuple-element.18) | copy-start | bytes 49156
  161.2 2.5 %copy-start.1 = (f32[32,128]{1,0:T(8,128)S(1)}, f32[32,128]{1,0:T(8,128)}, u32[]{:S(2)}) copy-start(f32[32,128]{1,0:T(8,128)} %get-tuple-element.19) | copy-start | bytes 49156
  161.2 3.1 %copy-start.3 = (f32[1,128]{1,0:T(1,128)S(1)}, f32[1,128]{1,0:T(1,128)}, u32[]{:S(2)}) copy-start(f32[1,128]{1,0:T(1,128)} %get-tuple-element.20) | copy-start | bytes 1540

commit v2 on v1

v2 whole, which is shorter than its diff:
```python
import jax
import jax.numpy as jnp
from jax import lax
from jax.experimental import pallas as pl
from jax.experimental.pallas import tpu as pltpu
from jax.sharding import PartitionSpec as P

MESH = pl.DeviceIdType.MESH
F32, BF16 = jnp.float32, jnp.bfloat16

TOK = 384
FF = 4096
D = 1024
W = 256
K = FF // W
DELTA = 1
LAG_D = 2
LAG_F = 6
RING = 8
WSLOT = 4
SOON = 3 * FF // 512
AHEAD = 6
OWN_W = 512
OWN = FF // OWN_W


def nt(left, right):
    return lax.dot_general(left, right, (((1,), (1,)), ((), ())), preferred_element_type=F32)


def kernel(
    tok_t, dy_t, hid_hbm, win_hbm, wout_hbm, row_in, col_in, row_out, col_out,
    gt_out, steps_out, new_row_in, new_col_in, new_row_out, new_col_out,
    steps, hid, win, wout_slot, wout_t, gath, dy, lhs, hgo, hgb, gtacc,
    f_send, f_recv, n_send, d_send, nd_recv, keep_d, keep_0,
    gs1, gr1, gs2, gk2, gr2, gs3, gk3, gr3,
    rb, rowm, colm, colr, rm1, rr1, rm2, rr2,
    load_sem, wout_sem, step_sem, z_ss, z_rs, s_ss, s_rs, y_ss, y_rs, c_ss, c_rs,
    x_ss, f_rs, nd_rs, g_ss, g_rs, e_ss, e_rs, l_ss, l_rs, r_ss, r_rs,
):
    dp = lax.axis_index("dp")
    mp = lax.axis_index("mp")
    zlo, x = dp // 4, dp % 4
    zhi, y, c = mp // 8, (mp // 2) % 4, mp % 2

    def dev(zlo_, x_, zhi_, y_, c_):
        return (zlo_ * 4 + x_, zhi_ * 8 + y_ * 2 + c_)

    x_peer = [dev(zlo, (x + i) % 4, zhi, y, c) for i in range(4)]
    y_peer = [dev(zlo, x, zhi, (y + i) % 4, c) for i in range(4)]
    zlo_peer = dev(1 - zlo, x, zhi, y, c)
    zhi_peer = dev(zlo, x, 1 - zhi, y, c)
    diag_peer = dev(1 - zlo, x, 1 - zhi, y, c)
    core_peer = dev(zlo, x, zhi, y, 1 - c)
    dp_peer = [((dp + i) % 8, mp) for i in range(8)]
    pair_peer = dev(zlo, x, 1 - zhi, y, 1 - c)

    def remote(src, dst, ss, rs, peer):
        return pltpu.make_async_remote_copy(
            src_ref=src, dst_ref=dst, send_sem=ss, recv_sem=rs, device_id=peer, device_id_type=MESH
        )

    loads = [
        pltpu.make_async_copy(hid_hbm, hid.at[pl.ds(zlo * TOK, TOK)], load_sem.at[0]),
        pltpu.make_async_copy(win_hbm, win, load_sem.at[1]),
    ]

    def wout_load(k):
        rows = pl.ds(pl.multiple_of(k * W, W), W)
        return pltpu.make_async_copy(wout_hbm.at[rows], wout_slot.at[k % WSLOT], wout_sem.at[k % WSLOT])

    for k in range(WSLOT):
        wout_load(k).start()
    for load in loads:
        load.start()

    barrier = pltpu.get_barrier_semaphore()
    peers = dp_peer[1:] + y_peer[1:] + [core_peer, zhi_peer, pair_peer, diag_peer]
    for peer in peers:
        pl.semaphore_signal(barrier, inc=1, device_id=peer, device_id_type=MESH)
    pl.semaphore_wait(barrier, len(peers))

    toks, dys = pl.ds(0, 64), pl.ds(64, 64)

    def s_copy(i):
        own, rows = (dy_t, dys) if i < 3 else (tok_t, toks)
        peer = (zlo_peer, diag_peer, zhi_peer)[i % 3]
        return remote(own, gath.at[zhi, y, c, zlo, rows], s_ss.at[i], s_rs.at[i], peer)

    far = (zhi + zlo) % 2

    def place(piece):
        if isinstance(piece, int) and piece >= 4:
            return zlo, piece - 4, toks
        second = piece // 2
        lo = (zlo + piece + second) % 2
        return (zhi + second) % 2, lo, dys

    def y_copy(piece, i):
        h, lo, rows = place(piece)
        part = gath.at[h, y, c, lo, rows]
        return remote(part, part, y_ss.at[piece], y_rs.at[piece], y_peer[i])

    def y_all(piece):
        h, lo, rows = place(piece)
        part = gath.at[h, pl.ds(0, 3), c, lo, rows]
        return remote(part, part, y_ss.at[piece], y_rs.at[piece], y_peer[1])

    def c_copy(piece):
        h, lo, rows = place(piece)
        part = gath.at[h, :, c, lo, rows]
        return remote(part, part, c_ss.at[piece], c_rs.at[piece], core_peer)

    def y_start(piece):
        for i in (1, 3, 2):
            y_copy(piece, i).start()

    def z_copy(k):
        cols = pl.ds(pl.multiple_of(k * W, W), W)
        return remote(
            hid_hbm.at[:, cols], hid.at[pl.ds(zlo * TOK, TOK), cols], z_ss.at[0], z_rs.at[k], zlo_peer
        )

    for i in (0, 1, 2):
        s_copy(i).start()
    gath[zhi, y, c, zlo, dys] = dy_t[...]
    y_start(0)

    @pl.when(far == 0)
    def _():
        s_copy(5).start()

    @pl.when(far == 1)
    def _():
        s_copy(3).start()
        s_copy(4).start()

    for k in range(AHEAD):
        z_copy(k).start()

    gath[zhi, y, c, zlo, toks] = tok_t[...]

    @pl.when(far == 0)
    def _():
        s_copy(0).wait_recv()
        y_start(1)
        s_copy(1).wait_recv()
        y_start(2)
        s_copy(2).wait_recv()
        y_start(3)

    @pl.when(far == 1)
    def _():
        s_copy(1).wait_recv()
        y_start(2)
        s_copy(2).wait_recv()
        y_start(3)
        s_copy(0).wait_recv()
        y_start(1)

    @pl.when(far == 0)
    def _():
        s_copy(3).wait_recv()

    @pl.when(far == 1)
    def _():
        s_copy(4).wait_recv()
        s_copy(5).wait_recv()

    y_start(4)
    y_start(5)

    def row_block(row):
        return jnp.broadcast_to(row[...], (128, 128)).T

    rb[0] = row_block(row_in)
    rb[1] = row_block(col_out)
    rowm[...] = jnp.zeros_like(rowm)

    def pass_to_core(piece):
        y_all(piece).wait_recv()
        c_copy(piece).start()

    def assemble(mat):
        for r in range(4):
            owner = (x + r) % 4
            for core in range(2):
                for lo in range(2):
                    lhs[mat, pl.ds(r * 128 + core * 64, 64), pl.ds(lo * TOK, TOK)] = gath[
                        zlo, owner, core, lo, pl.ds(64 * mat, 64), :
                    ]

    def transpose_dy():
        for h in range(2):
            for yy in range(4):
                for lo in range(2):
                    both = jnp.concatenate(
                        [gath[h, yy, 0, lo, 64:128, :], gath[h, yy, 1, lo, 64:128, :]], axis=0
                    )
                    dy[pl.ds(lo * TOK, TOK), pl.ds((h * 4 + yy) * 128, 128)] = both.astype(F32).T.astype(BF16)

    def transpose_wout(k, carry):
        wout_load(k).wait()
        cols = pl.ds(pl.multiple_of(k * W, W), W)
        wout_t[:, cols] = wout_slot[k % WSLOT].T

        @pl.when(k + WSLOT < K)
        def _():
            wout_load(k + WSLOT).start()

        return carry

    lax.fori_loop(0, K // 2, transpose_wout, 0)
    first, rest = 2 * far, 2 * (1 - far)
    pass_to_core(first)
    pass_to_core(first + 1)
    c_copy(first).wait_recv()
    c_copy(first + 1).wait_recv()
    assemble(1)
    loads[0].wait()

    toward = [(x_peer[1], x_peer[3]), (x_peer[3], x_peer[1])]

    def f_copy(mat, k):
        return remote(f_send.at[mat, k], f_recv.at[mat, k], x_ss.at[0], f_rs.at[mat, k], toward[mat][0])

    def n_copy(mat, k):
        return remote(n_send.at[mat, k], nd_recv.at[mat, k, 0], x_ss.at[1], nd_rs.at[mat, k], toward[mat][1])

    def d_copy(mat, k):
        return remote(d_send.at[mat, k], nd_recv.at[mat, k, 1], x_ss.at[2], nd_rs.at[mat, k], toward[mat][0])

    def products(mat, k, right):
        part = jnp.dot(lhs[mat], right, preferred_element_type=F32)
        near, back = (3, 1) if mat == 0 else (1, 3)
        slot = k % RING
        f_send[mat, k] = part[256:384].astype(BF16)
        f_copy(mat, k).start()
        n_send[mat, k] = part[near * 128 : near * 128 + 128].astype(BF16)
        n_copy(mat, k).start()
        keep_d[mat, slot] = part[back * 128 : back * 128 + 128]
        keep_0[mat, slot] = part[0:128]

    def pass_on(mat, k):
        f_copy(mat, k).wait_recv()
        d_send[mat, k] = (keep_d[mat, k % RING] + f_recv[mat, k].astype(F32)).astype(BF16)
        d_copy(mat, k).start()

    def step_copy(mat, k):
        cols = pl.ds(pl.multiple_of(k * W, W), W)
        return pltpu.make_async_copy(steps.at[mat, :, cols], steps_out.at[mat, :, cols], step_sem.at[0])

    def finish(mat, k):
        both = nd_recv.at[mat, k]
        remote(both, both, x_ss.at[1], nd_rs.at[mat, k], toward[mat][1]).wait_recv()
        lanes = col_in if mat == 0 else row_out
        for h in range(W // 128):
            cut = pl.ds(h * 128, 128)
            g = (
                keep_0[mat, k % RING, :, cut]
                + nd_recv[mat, k, 0, :, cut].astype(F32)
                + nd_recv[mat, k, 1, :, cut].astype(F32)
            )
            block = k * (W // 128) + h
            nu = jnp.minimum(rb[mat], lanes[pl.ds(block, 1), :]) + g * g
            step = g * lax.rsqrt(nu)
            steps[mat, :, pl.ds(pl.multiple_of(block * 128, 128), 128)] = step.astype(BF16)
            rowm[mat] = jnp.maximum(rowm[mat], nu)
            last = block // SOON
            row = (1 - mat) * (SOON - last * (2 * SOON - FF // 128)) + last * SOON + block
            colm[pl.ds(row, 1), :] = jnp.max(nu, axis=0, keepdims=True)
        step_copy(mat, k).start()

    def hidden_grad(lo, start, width):
        cols = pl.ds(pl.multiple_of(start, width), width)
        rows = pl.ds(pl.multiple_of(lo * TOK, TOK), TOK)
        back = jnp.dot(dy[rows, :], wout_t[:, cols], preferred_element_type=F32)
        return jnp.where(hid[rows, cols] > 0, back, F32(0.0)).astype(BF16)

    def own_tokens(j):
        cols = pl.ds(pl.multiple_of(j * OWN_W, OWN_W), OWN_W)
        grad = hidden_grad(zlo, j * OWN_W, OWN_W)
        hgo[:, cols] = grad
        gtacc[...] += nt(win[:, cols], grad)

    def g_copy(i):
        if i == 0:
            return remote(gs1, gr1, g_ss.at[0], g_rs.at[0], core_peer)
        if i < 4:
            return remote(gs2.at[(y + i) % 4], gr2.at[i - 1], g_ss.at[1], g_rs.at[1], y_peer[i])
        return remote(gs3, gr3, g_ss.at[2], g_rs.at[2], zhi_peer)

    def g_all():
        return remote(gs2.at[pl.ds(0, 3)], gr2, g_ss.at[1], g_rs.at[1], y_peer[1])

    def gt_rows(j, core):
        return gtacc[pl.ds(pl.multiple_of(j * 128 + core * 64, 64), 64), :]

    def gt_stage(i):
        if i == 0:
            for j in range(8):
                gs1[j] = gt_rows(j, 1 - c).astype(BF16)
            g_copy(0).start()
        elif i == 1:
            g_copy(0).wait_recv()
            for h in range(2):
                for yy in range(4):
                    gs2[yy, h] = (gt_rows(h * 4 + yy, c) + gr1[h * 4 + yy].astype(F32)).astype(BF16)
                gk2[h] = gt_rows(h * 4 + y, c) + gr1[h * 4 + y].astype(F32)
            for j in (1, 2, 3):
                g_copy(j).start()
        elif i == 2:
            g_all().wait_recv()

            def total(h):
                return gk2[h] + gr2[0, h].astype(F32) + gr2[1, h].astype(F32) + gr2[2, h].astype(F32)

            gs3[...] = total(1 - zhi).astype(BF16)
            gk3[...] = total(zhi)
            g_copy(4).start()
        else:
            g_copy(4).wait_recv()
            gt_out[...] = (gk3[...] + gr3[...].astype(F32)).astype(BF16)
            g_copy(0).wait_send()
            g_all().wait_send()
            g_copy(4).wait_send()

    def between(value, low, high):
        return jnp.logical_and(value >= low, value < high)

    early, late = pl.ds(0, 2 * SOON), pl.ds(2 * SOON, 2 * FF // 128 - 2 * SOON)

    def early_copy(i):
        return remote(colm.at[early], colr.at[i - 1, early], e_ss.at[0], e_rs.at[0], dp_peer[i])

    def late_copy(i):
        return remote(colm.at[late], colr.at[i - 1, late], l_ss.at[0], l_rs.at[0], dp_peer[i])

    def turn(i, carry):
        for mat, first in ((1, 0), (0, DELTA)):

            @pl.when(between(i - first - LAG_D, 0, K))
            def _():
                pass_on(mat, i - first - LAG_D)

            @pl.when(between(i - first - LAG_F, 0, K))
            def _():
                finish(mat, i - first - LAG_F)

        @pl.when(i < K)
        def _():
            z_copy(i).wait_recv()

            @pl.when(i + AHEAD < K)
            def _():
                z_copy(i + AHEAD).start()

            cols = pl.ds(pl.multiple_of(i * W, W), W)
            pre = hid[:, cols]
            products(1, i, jnp.maximum(pre, jnp.zeros_like(pre)))

        p = i - DELTA

        @pl.when(p == 0)
        def _():
            for piece in (rest, rest + 1, 4, 5):
                pass_to_core(piece)
            c_copy(rest).wait_recv()
            c_copy(rest + 1).wait_recv()
            lax.fori_loop(K // 2, K, transpose_wout, 0)
            transpose_dy()
            c_copy(4).wait_recv()
            c_copy(5).wait_recv()
            assemble(0)
            loads[1].wait()
            gtacc[...] = jnp.zeros_like(gtacc)

        @pl.when(between(p, 0, OWN))
        def _():
            own_tokens(p)

        @pl.when(between(p, 0, K))
        def _():
            cols = pl.ds(pl.multiple_of(p * W, W), W)
            hgb[pl.ds(pl.multiple_of(zlo * TOK, TOK), TOK), :] = hgo[:, cols]
            hgb[pl.ds(pl.multiple_of((1 - zlo) * TOK, TOK), TOK), :] = hidden_grad(1 - zlo, p * W, W)
            products(0, p, hgb[...])

        for s, at in enumerate((OWN, OWN + 1, OWN + 3, OWN + 5)):

            @pl.when(p == at)
            def _():
                gt_stage(s)

        @pl.when(i == K * 3 // 4 - 1 + DELTA + LAG_F)
        def _():
            for j in range(1, 8):
                early_copy(j).start()

        return carry

    lax.fori_loop(0, K + DELTA + LAG_F, turn, 0)

    for i in range(1, 8):
        late_copy(i).start()
    rm1[...] = jnp.zeros_like(rm1)
    for mat in range(2):
        rm1[mat : mat + 1, :] = jnp.max(rowm[mat].T, axis=0, keepdims=True)

    def row_copy(i):
        if i < 3:
            return remote(rm1, rr1.at[i], r_ss.at[0], r_rs.at[0], (core_peer, zhi_peer, pair_peer)[i])
        return remote(rm2, rr2.at[i - 3], r_ss.at[1], r_rs.at[1], y_peer[i - 2])

    for i in range(3):
        row_copy(i).start()
    row_1 = remote(rr1, rr1, r_ss.at[0], r_rs.at[0], core_peer)
    row_2 = remote(rr2, rr2, r_ss.at[1], r_rs.at[1], y_peer[1])
    row_1.wait_recv()
    rm2[...] = jnp.maximum(jnp.maximum(rm1[...], rr1[0]), jnp.maximum(rr1[1], rr1[2]))
    for i in range(3, 6):
        row_copy(i).start()

    for i in range(3):
        s_copy(i).wait_send()

    @pl.when(far == 0)
    def _():
        s_copy(5).wait_send()

    @pl.when(far == 1)
    def _():
        s_copy(3).wait_send()
        s_copy(4).wait_send()

    for piece in range(6):
        y_all(piece).wait_send()
        c_copy(piece).wait_send()

    own_rows = hid.at[pl.ds(zlo * TOK, TOK)]
    remote(hid_hbm, own_rows, z_ss.at[0], z_rs.at[0], zlo_peer).wait_send()
    remote(f_send, f_recv, x_ss.at[0], f_rs.at[0, 0], x_peer[1]).wait_send()
    remote(n_send, f_recv, x_ss.at[1], f_rs.at[0, 0], x_peer[1]).wait_send()
    remote(d_send, f_recv, x_ss.at[2], f_rs.at[0, 0], x_peer[1]).wait_send()

    pltpu.make_async_copy(steps, steps_out, step_sem.at[0]).wait()

    remote(colr.at[:, early], colr.at[:, early], e_ss.at[0], e_rs.at[0], zlo_peer).wait()
    remote(colr.at[:, late], colr.at[:, late], l_ss.at[0], l_rs.at[0], zlo_peer).wait()
    top = colm[...]
    for i in range(7):
        top = jnp.maximum(top, colr[i])
    rest_rows = FF // 128 - SOON
    new_row_out[...] = jnp.concatenate([top[0:SOON], top[2 * SOON : 2 * SOON + rest_rows]], axis=0)
    new_col_in[...] = jnp.concatenate([top[SOON : 2 * SOON], top[2 * SOON + rest_rows :]], axis=0)
    row_1.wait_send()
    row_2.wait()
    top = jnp.maximum(jnp.maximum(rm2[...], rr2[0]), jnp.maximum(rr2[1], rr2[2]))
    new_row_in[...] = top[0:1]
    new_col_out[...] = top[1:2]


def write_out(steps_in, steps_out, gt, nri, nci, nro, nco, o_gt, o_in, o_out, o_nri, o_nci, o_nro, o_nco):
    o_in[...] = steps_in[0].astype(F32)
    o_out[...] = steps_out[0].astype(F32).T

    @pl.when(pl.program_id(0) == 0)
    def _():
        o_gt[...] = gt[...]
        o_nri[...] = nri[...]
        o_nci[...] = nci[...]
        o_nro[...] = nro[...]
        o_nco[...] = nco[...]


def on_device(tokens, grad_out, hidden_pre, w_in, w_out, row_in, col_in, row_out, col_out):
    vmem = pl.BlockSpec(memory_space=pltpu.VMEM)
    hbm = pl.BlockSpec(memory_space=pl.ANY)
    dma = pltpu.SemaphoreType.DMA
    rows = FF // 128
    wire = pltpu.VMEM((2, K, 128, W), BF16)
    kept = pltpu.VMEM((2, RING, 128, W), F32)
    small = (
        jax.ShapeDtypeStruct((64, TOK), BF16),
        jax.ShapeDtypeStruct((1, 128), F32),
        jax.ShapeDtypeStruct((rows, 128), F32),
        jax.ShapeDtypeStruct((rows, 128), F32),
        jax.ShapeDtypeStruct((1, 128), F32),
    )
    gt, steps, nri, nci, nro, nco = pl.pallas_call(
        kernel,
        out_shape=small[:1] + (jax.ShapeDtypeStruct((2, 128, FF), BF16),) + small[1:],
        in_specs=[vmem, vmem, hbm, hbm, hbm, vmem, vmem, vmem, vmem],
        out_specs=(vmem, hbm, vmem, vmem, vmem, vmem),
        scratch_shapes=[
            pltpu.VMEM((2, 128, FF), BF16),
            pltpu.VMEM((2 * TOK, FF), BF16),
            pltpu.VMEM((D, FF), BF16),
            pltpu.VMEM((WSLOT, W, D), BF16),
            pltpu.VMEM((D, FF), BF16),
            pltpu.VMEM((2, 4, 2, 2, 128, TOK), BF16),
            pltpu.VMEM((2 * TOK, D), BF16),
            pltpu.VMEM((2, 512, 2 * TOK), BF16),
            pltpu.VMEM((TOK, FF), BF16),
            pltpu.VMEM((2 * TOK, W), BF16),
            pltpu.VMEM((D, TOK), F32),
            wire, wire, wire, wire,
            pltpu.VMEM((2, K, 2, 128, W), BF16),
            kept, kept,
            pltpu.VMEM((8, 64, TOK), BF16),
            pltpu.VMEM((8, 64, TOK), BF16),
            pltpu.VMEM((4, 2, 64, TOK), BF16),
            pltpu.VMEM((2, 64, TOK), F32),
            pltpu.VMEM((3, 2, 64, TOK), BF16),
            pltpu.VMEM((64, TOK), BF16),
            pltpu.VMEM((64, TOK), F32),
            pltpu.VMEM((64, TOK), BF16),
            pltpu.VMEM((2, 128, 128), F32),
            pltpu.VMEM((2, 128, 128), F32),
            pltpu.VMEM((2 * rows, 128), F32),
            pltpu.VMEM((7, 2 * rows, 128), F32),
            pltpu.VMEM((8, 128), F32),
            pltpu.VMEM((3, 8, 128), F32),
            pltpu.VMEM((8, 128), F32),
            pltpu.VMEM((3, 8, 128), F32),
            dma((2,)), dma((WSLOT,)), dma((1,)),
            dma((1,)), dma((K,)),
            dma((6,)), dma((6,)),
            dma((6,)), dma((6,)),
            dma((6,)), dma((6,)),
            dma((3,)), dma((2, K)), dma((2, K)),
            dma((3,)), dma((3,)),
            dma((1,)), dma((1,)),
            dma((1,)), dma((1,)),
            dma((2,)), dma((2,)),
        ],
        compiler_params=pltpu.CompilerParams(
            collective_id=0, has_side_effects=True, vmem_limit_bytes=63 * 2**20
        ),
        name="ffn_backward",
    )(
        tokens.T, grad_out.T, hidden_pre, w_in, w_out,
        row_in.reshape(1, 128), col_in.reshape(rows, 128), row_out.reshape(rows, 128), col_out.reshape(1, 128),
    )

    parts = 2
    wide = FF // parts

    def whole(shape):
        return pl.BlockSpec(shape.shape, lambda j: (0,) * len(shape.shape))

    gt, step_in, step_out, nri, nci, nro, nco = pl.pallas_call(
        write_out,
        grid=(parts,),
        out_shape=small[:1]
        + (jax.ShapeDtypeStruct((128, FF), F32), jax.ShapeDtypeStruct((FF, 128), F32))
        + small[1:],
        in_specs=[
            pl.BlockSpec((1, 128, wide), lambda j: (0, 0, j)),
            pl.BlockSpec((1, 128, wide), lambda j: (1, 0, j)),
        ]
        + [whole(shape) for shape in small],
        out_specs=(
            whole(small[0]),
            pl.BlockSpec((128, wide), lambda j: (0, j)),
            pl.BlockSpec((wide, 128), lambda j: (j, 0)),
        )
        + tuple(whole(shape) for shape in small[1:]),
        name="write_out",
    )(steps, steps, gt, nri, nci, nro, nco)
    return (
        gt.T, step_in, step_out,
        nri.reshape(128), nci.reshape(FF), nro.reshape(FF), nco.reshape(128),
    )


def solution(mesh):
    in_specs = (
        P("dp", "mp"),
        P("dp", "mp"),
        P("dp", "mp"),
        P(None, "mp"),
        P("mp", None),
        P("dp"),
        P("mp"),
        P("mp"),
        P("dp"),
    )
    out_specs = (P("dp", "mp"), P("dp", "mp"), P("mp", "dp"), P("dp"), P("mp"), P("mp"), P("dp"))
    return jax.shard_map(
        on_device, mesh=mesh, in_specs=in_specs, out_specs=out_specs, check_vma=False
    )
```

time: 165 us -> 111 us (0.67)
  Pallas kernels: 154 us -> 109 us
  local copies, waits for them, and re-layouts: 8.26 us -> 0 us
    pallas_call x1 -> x2, Pallas kernels: 154 us -> 109 us  [the longest x1 106 us: on_device(): pl.pallas_call(kernel, out_shape=small[:1] + (jax.ShapeDtypeStruct((2, 12...]
    unnamed x17 -> x0, local copies, waits for them, and re-layouts: 8.26 us -> none
where the time goes in v2:
time: 111 us; the launch traced here: 110 us
  Pallas kernels  109 us (98%)
    pallas_call x1, Pallas kernels, on_device(): pl.pallas_call(kernel, out_shape=small[:1] + (jax.ShapeDtypeStruct((2, 12...  106 us
    pallas_call x1, Pallas kernels, on_device(): pl.pallas_call(write_out, grid=(parts,), out_shape=small[:1] + (jax.Shape...  3.51 us

profile of v2, /device:TPU:0, one launch (start us, length us, event | category | flops | bytes accessed | tf_op | source)
XLA Modules:
  0.0 110.0 jit_solution(15146790222248740411)
XLA Ops:
  0.6 105.8 %ffn_backward.1 = (bf16[64,384]{1,0:T(8,128)(2,1)}, bf16[2,128,4096]{2,1,0:T(8,128)(2,1)}, f32[1,128]{1,0:T(1,128)}, f32[32,128]{1,0:T(8,128)}, f32[32,128]{1,0:T(8,128)}, /*index=5*/f32[1,128]{1,0:T(1,128)}) custom-call(bf16[64,384]{1,0:T(8,128)(2,1)} %bitcast.11, bf16[64,384]{1,0:T(8,128)(2,1)} %bitcast.12, bf16[384,4096]{1,0:T(8,128)(2,1)} %hid_hbm.1, ...), custom_call_target="tpu_custom_call" | custom-call | tf_op jit(solution)/shard_map/ffn_backward/pallas_call | solution.py:490
  106.5 3.5 %write_out.1 = (bf16[64,384]{1,0:T(8,128)(2,1)}, f32[128,4096]{1,0:T(8,128)}, f32[4096,128]{1,0:T(8,128)}, f32[1,128]{1,0:T(1,128)}, f32[32,128]{1,0:T(8,128)}, /*index=5*/f32[32,128]{1,0:T(8,128)}, f32[1,128]{1,0:T(1,128)}) custom-call(bf16[2,128,4096]{2,1,0:T(8,128)(2,1)} %get-tuple-element.20.steps_in.steps_out, ...), custom_call_target="tpu_custom_call" | custom-call | tf_op jit(solution)/shard_map/write_out/pallas_call | solution.py:552

commit v3 on v2

--- a/solution.py
+++ b/solution.py
@@ -15,7 +15,7 @@
 K = FF // W
 DELTA = 1
 LAG_D = 2
-LAG_F = 6
+LAG_F = 5
 RING = 8
 WSLOT = 4
 SOON = 3 * FF // 512
@@ -34,9 +34,9 @@
     steps, hid, win, wout_slot, wout_t, gath, dy, lhs, hgo, hgb, gtacc,
     f_send, f_recv, n_send, d_send, nd_recv, keep_d, keep_0,
     gs1, gr1, gs2, gk2, gr2, gs3, gk3, gr3,
-    rb, rowm, colm, colr, rm1, rr1, rm2, rr2,
+    rb, rowm, colm, colz, colm2, colr, rm1, rr1, rm2, rr2,
     load_sem, wout_sem, step_sem, z_ss, z_rs, s_ss, s_rs, y_ss, y_rs, c_ss, c_rs,
-    x_ss, f_rs, nd_rs, g_ss, g_rs, e_ss, e_rs, l_ss, l_rs, r_ss, r_rs,
+    x_ss, f_rs, nd_rs, g_ss, g_rs, e_ss, e_rs, r_ss, r_rs,
 ):
     dp = lax.axis_index("dp")
     mp = lax.axis_index("mp")
@@ -52,7 +52,6 @@
     zhi_peer = dev(zlo, x, 1 - zhi, y, c)
     diag_peer = dev(1 - zlo, x, 1 - zhi, y, c)
     core_peer = dev(zlo, x, zhi, y, 1 - c)
-    dp_peer = [((dp + i) % 8, mp) for i in range(8)]
     pair_peer = dev(zlo, x, 1 - zhi, y, 1 - c)
 
     def remote(src, dst, ss, rs, peer):
@@ -75,7 +74,7 @@
         load.start()
 
     barrier = pltpu.get_barrier_semaphore()
-    peers = dp_peer[1:] + y_peer[1:] + [core_peer, zhi_peer, pair_peer, diag_peer]
+    peers = x_peer[1:] + y_peer[1:] + [core_peer, zlo_peer, zhi_peer, pair_peer, diag_peer]
     for peer in peers:
         pl.semaphore_signal(barrier, inc=1, device_id=peer, device_id_type=MESH)
     pl.semaphore_wait(barrier, len(peers))
@@ -112,7 +111,7 @@
         return remote(part, part, c_ss.at[piece], c_rs.at[piece], core_peer)
 
     def y_start(piece):
-        for i in (1, 3, 2):
+        for i in (2, 1, 3):
             y_copy(piece, i).start()
 
     def z_copy(k):
@@ -277,11 +276,13 @@
         back = jnp.dot(dy[rows, :], wout_t[:, cols], preferred_element_type=F32)
         return jnp.where(hid[rows, cols] > 0, back, F32(0.0)).astype(BF16)
 
-    def own_tokens(j):
+    def own_grad(j):
         cols = pl.ds(pl.multiple_of(j * OWN_W, OWN_W), OWN_W)
-        grad = hidden_grad(zlo, j * OWN_W, OWN_W)
-        hgo[:, cols] = grad
-        gtacc[...] += nt(win[:, cols], grad)
+        hgo[:, cols] = hidden_grad(zlo, j * OWN_W, OWN_W)
+
+    def own_term(j):
+        cols = pl.ds(pl.multiple_of(j * OWN_W, OWN_W), OWN_W)
+        gtacc[...] += nt(win[:, cols], hgo[:, cols])
 
     def g_copy(i):
         if i == 0:
@@ -330,11 +331,20 @@
 
     early, late = pl.ds(0, 2 * SOON), pl.ds(2 * SOON, 2 * FF // 128 - 2 * SOON)
 
-    def early_copy(i):
-        return remote(colm.at[early], colr.at[i - 1, early], e_ss.at[0], e_rs.at[0], dp_peer[i])
-
-    def late_copy(i):
-        return remote(colm.at[late], colr.at[i - 1, late], l_ss.at[0], l_rs.at[0], dp_peer[i])
+    def col_pair(part, j):
+        return remote(colm.at[part], colz.at[part], e_ss.at[j], e_rs.at[j], zlo_peer)
+
+    def col_ring(part, j, i):
+        return remote(colm2.at[part], colr.at[i - 1, part], e_ss.at[2 + j], e_rs.at[2 + j], x_peer[i])
+
+    def col_all(part, j):
+        return remote(colr.at[:, part], colr.at[:, part], e_ss.at[2 + j], e_rs.at[2 + j], x_peer[1])
+
+    def pass_columns(part, j):
+        col_pair(part, j).wait()
+        colm2[part] = jnp.maximum(colm[part], colz[part])
+        for i in (2, 1, 3):
+            col_ring(part, j, i).start()
 
     def turn(i, carry):
         for mat, first in ((1, 0), (0, DELTA)):
@@ -363,28 +373,43 @@
 
         @pl.when(p == 0)
         def _():
-            for piece in (rest, rest + 1, 4, 5):
-                pass_to_core(piece)
+            pass_to_core(rest)
+            pass_to_core(rest + 1)
             c_copy(rest).wait_recv()
             c_copy(rest + 1).wait_recv()
-            lax.fori_loop(K // 2, K, transpose_wout, 0)
             transpose_dy()
+            pass_to_core(4)
+            pass_to_core(5)
+
+        @pl.when(between(p, 0, OWN))
+        def _():
+            own_grad(p)
+
+        @pl.when(between(p, 0, K))
+        def _():
+            cols = pl.ds(pl.multiple_of(p * W, W), W)
+            hgb[pl.ds(pl.multiple_of(zlo * TOK, TOK), TOK), :] = hgo[:, cols]
+            hgb[pl.ds(pl.multiple_of((1 - zlo) * TOK, TOK), TOK), :] = hidden_grad(1 - zlo, p * W, W)
+
+        @pl.when(p == 0)
+        def _():
             c_copy(4).wait_recv()
             c_copy(5).wait_recv()
             assemble(0)
+
+        @pl.when(between(p, 0, K))
+        def _():
+            products(0, p, hgb[...])
+
+        @pl.when(p == 0)
+        def _():
             loads[1].wait()
             gtacc[...] = jnp.zeros_like(gtacc)
+            lax.fori_loop(K // 2, K, transpose_wout, 0)
 
         @pl.when(between(p, 0, OWN))
         def _():
-            own_tokens(p)
-
-        @pl.when(between(p, 0, K))
-        def _():
-            cols = pl.ds(pl.multiple_of(p * W, W), W)
-            hgb[pl.ds(pl.multiple_of(zlo * TOK, TOK), TOK), :] = hgo[:, cols]
-            hgb[pl.ds(pl.multiple_of((1 - zlo) * TOK, TOK), TOK), :] = hidden_grad(1 - zlo, p * W, W)
-            products(0, p, hgb[...])
+            own_term(p)
 
         for s, at in enumerate((OWN, OWN + 1, OWN + 3, OWN + 5)):
 
@@ -394,15 +419,17 @@
 
         @pl.when(i == K * 3 // 4 - 1 + DELTA + LAG_F)
         def _():
-            for j in range(1, 8):
-                early_copy(j).start()
+            col_pair(early, 0).start()
+
+        @pl.when(i == K * 3 // 4 + 1 + DELTA + LAG_F)
+        def _():
+            pass_columns(early, 0)
 
         return carry
 
     lax.fori_loop(0, K + DELTA + LAG_F, turn, 0)
 
-    for i in range(1, 8):
-        late_copy(i).start()
+    col_pair(late, 1).start()
     rm1[...] = jnp.zeros_like(rm1)
     for mat in range(2):
         rm1[mat : mat + 1, :] = jnp.max(rowm[mat].T, axis=0, keepdims=True)
@@ -412,13 +439,14 @@
             return remote(rm1, rr1.at[i], r_ss.at[0], r_rs.at[0], (core_peer, zhi_peer, pair_peer)[i])
         return remote(rm2, rr2.at[i - 3], r_ss.at[1], r_rs.at[1], y_peer[i - 2])
 
-    for i in range(3):
+    for i in (2, 1, 0):
         row_copy(i).start()
     row_1 = remote(rr1, rr1, r_ss.at[0], r_rs.at[0], core_peer)
     row_2 = remote(rr2, rr2, r_ss.at[1], r_rs.at[1], y_peer[1])
+    pass_columns(late, 1)
     row_1.wait_recv()
     rm2[...] = jnp.maximum(jnp.maximum(rm1[...], rr1[0]), jnp.maximum(rr1[1], rr1[2]))
-    for i in range(3, 6):
+    for i in (4, 3, 5):
         row_copy(i).start()
 
     for i in range(3):
@@ -445,10 +473,10 @@
 
     pltpu.make_async_copy(steps, steps_out, step_sem.at[0]).wait()
 
-    remote(colr.at[:, early], colr.at[:, early], e_ss.at[0], e_rs.at[0], zlo_peer).wait()
-    remote(colr.at[:, late], colr.at[:, late], l_ss.at[0], l_rs.at[0], zlo_peer).wait()
-    top = colm[...]
-    for i in range(7):
+    col_all(early, 0).wait()
+    col_all(late, 1).wait()
+    top = colm2[...]
+    for i in range(3):
         top = jnp.maximum(top, colr[i])
     rest_rows = FF // 128 - SOON
     new_row_out[...] = jnp.concatenate([top[0:SOON], top[2 * SOON : 2 * SOON + rest_rows]], axis=0)
@@ -518,7 +546,9 @@
             pltpu.VMEM((2, 128, 128), F32),
             pltpu.VMEM((2, 128, 128), F32),
             pltpu.VMEM((2 * rows, 128), F32),
-            pltpu.VMEM((7, 2 * rows, 128), F32),
+            pltpu.VMEM((2 * rows, 128), F32),
+            pltpu.VMEM((2 * rows, 128), F32),
+            pltpu.VMEM((3, 2 * rows, 128), F32),
             pltpu.VMEM((8, 128), F32),
             pltpu.VMEM((3, 8, 128), F32),
             pltpu.VMEM((8, 128), F32),
@@ -530,8 +560,7 @@
             dma((6,)), dma((6,)),
             dma((3,)), dma((2, K)), dma((2, K)),
             dma((3,)), dma((3,)),
-            dma((1,)), dma((1,)),
-            dma((1,)), dma((1,)),
+            dma((4,)), dma((4,)),
             dma((2,)), dma((2,)),
         ],
         compiler_params=pltpu.CompilerParams(

time: 111 us -> 109 us (0.982); the launches traced: 110 us -> 109 us
  no operation moved by 1% of the time
where the time goes in v3:
time: 109 us
  Pallas kernels  109 us (100%)
    pallas_call x1, Pallas kernels, on_device(): pl.pallas_call(kernel, out_shape=small[:1] + (jax.ShapeDtypeStruct((2, 12...  105 us
    pallas_call x1, Pallas kernels, on_device(): pl.pallas_call(write_out, grid=(parts,), out_shape=small[:1] + (jax.Shape...  3.51 us

profile of v3, /device:TPU:0, one launch (start us, length us, event | category | flops | bytes accessed | tf_op | source)
XLA Modules:
  0.0 109.2 jit_solution(17428928451509009331)
XLA Ops:
  0.6 105.0 %ffn_backward.1 = (bf16[64,384]{1,0:T(8,128)(2,1)}, bf16[2,128,4096]{2,1,0:T(8,128)(2,1)}, f32[1,128]{1,0:T(1,128)}, f32[32,128]{1,0:T(8,128)}, f32[32,128]{1,0:T(8,128)}, /*index=5*/f32[1,128]{1,0:T(1,128)}) custom-call(bf16[64,384]{1,0:T(8,128)(2,1)} %bitcast.11, bf16[64,384]{1,0:T(8,128)(2,1)} %bitcast.12, bf16[384,4096]{1,0:T(8,128)(2,1)} %hid_hbm.1, ...), custom_call_target="tpu_custom_call" | custom-call | tf_op jit(solution)/shard_map/ffn_backward/pallas_call | solution.py:518
  105.7 3.5 %write_out.1 = (bf16[64,384]{1,0:T(8,128)(2,1)}, f32[128,4096]{1,0:T(8,128)}, f32[4096,128]{1,0:T(8,128)}, f32[1,128]{1,0:T(1,128)}, f32[32,128]{1,0:T(8,128)}, /*index=5*/f32[32,128]{1,0:T(8,128)}, f32[1,128]{1,0:T(1,128)}) custom-call(bf16[2,128,4096]{2,1,0:T(8,128)(2,1)} %get-tuple-element.20.steps_in.steps_out, ...), custom_call_target="tpu_custom_call" | custom-call | tf_op jit(solution)/shard_map/write_out/pallas_call | solution.py:581
